TPU v7x, 32 devices: a whole 2x2x4 slice. The times are simulated.
32 devices in a mesh: energy: 2 (over x), atom: 4 (over y, core), orb: 4 (over z).
Axes of the slice: x: 2, y: 2, z: 4, core: 2. Of those that a mesh axis runs over, the one named last changes fastest.
Arguments:
- green_lesser: bfloat16 [8, 4, 64, 128], P(('energy', 'atom'), None, 'orb'), may hold values from -6 to 6
- occupation: float32 [2], replicated, may hold values from 0.1 to 2
- coupling_blocks: bfloat16 [32, 2, 64, 64], replicated, may hold values from -0.375 to 0.375
- neighbours: int32 [4, 8], P('atom'), may hold values from 0 to 3, as said below
- coupling_index: int32 [4, 8], P('atom'), may hold values from 0 to 31
- neighbour_count: int32 [4], P('atom'), may hold values from 2 to 8, as said below
Outputs:
- sigma_lesser: bfloat16 [8, 4, 64, 128], P(('energy', 'atom'), None, 'orb')
Inputs may be any that keep to these rules, and one draw needn't show every extreme that they name: `neighbours`: row a lists atoms at most 1 positions from atom a; repeats are allowed. Slots p with p >= neighbour_count[a] are unused.
All inputs are finite; a program needn't handle non-finite values.
Results may differ from a plain program's by a relative error of at most 0.0057.
Values may be sent and summed in bfloat16 or wider, within the bound.
No kernel may reach another device: no remote copies, remote signals or barrier semaphores. Data moves between devices by JAX's collectives and lax.ppermute only.
A program may use at most 64 MiB of HBM per device.

v0:
```python
import jax
import jax.numpy as jnp
from jax import lax
from jax.sharding import PartitionSpec as P

SHIFT_LO = 2
SHIFT_HI = 4


def extended(shard, sides, width):
    for axis, dim in sides:
        peers, length = (lax.axis_size(axis), shard.shape[dim])
        up = [(i, (i + 1) % peers) for i in range(peers - 1)]
        down = [(j, i) for i, j in up]
        last = lax.slice_in_dim(shard, length - width, length, axis=dim)
        initial = lax.slice_in_dim(shard, 0, width, axis=dim)
        before = lax.ppermute(last, axis, up)
        after = lax.ppermute(initial, axis, down)
        shard = jnp.concatenate([before, shard, after], axis=dim)
    return shard


def lesser_terms(haloed, local_index, weights, couplings, occupation, margin, column_start):
    picked = jnp.take(haloed, local_index, axis=1)
    energy_rows = haloed.shape[0] - 2 * margin
    atom_rows, slot_count = local_index.shape
    column_count = haloed.shape[2]
    orbital = couplings.shape[-1]
    running = jnp.zeros((energy_rows, atom_rows, orbital, haloed.shape[3]), jnp.float32)
    for phonon, shift_size in enumerate((SHIFT_LO, SHIFT_HI)):
        below_rows = picked[margin - shift_size : margin - shift_size + energy_rows].astype(
            jnp.float32
        )
        above_rows = picked[margin + shift_size : margin + shift_size + energy_rows].astype(
            jnp.float32
        )
        combined = (
            occupation[phonon] * below_rows + (occupation[phonon] + 1.0) * above_rows
        ) * weights[None, :, :, None, None]
        combined = combined.astype(jnp.bfloat16).reshape(
            energy_rows, atom_rows, slot_count, column_count, 2, orbital
        )
        matrices = couplings[:, :, phonon]
        left_product = jnp.einsum(
            "eapjck,apik->eapjci", combined, matrices, preferred_element_type=jnp.float32
        )
        left_product = left_product.astype(jnp.bfloat16).reshape(
            energy_rows, atom_rows, slot_count, column_count, 2 * orbital
        )
        column_part = lax.dynamic_slice_in_dim(matrices, column_start, column_count, 3)
        running = running + jnp.einsum(
            "aplj,eapjx->ealx", column_part, left_product, preferred_element_type=jnp.float32
        )
    return running


def body(green_lesser, occupation, coupling_blocks, neighbours, coupling_index, neighbour_count):
    atom_rows, slot_count = neighbours.shape
    slot_index = lax.broadcasted_iota(jnp.int32, (atom_rows, slot_count), 1)
    weights = (slot_index < neighbour_count[:, None]).astype(jnp.float32)
    local_index = neighbours - lax.axis_index("atom") * atom_rows + atom_rows
    couplings = jnp.take(coupling_blocks, coupling_index, axis=0)
    by_atoms = lax.all_to_all(green_lesser, "atom", split_axis=1, concat_axis=0, tiled=True)
    widened = extended(by_atoms, (("energy", 0),), SHIFT_HI)
    haloed = extended(widened, (("atom", 1),), atom_rows)
    column_start = lax.axis_index("orb") * haloed.shape[2]
    running = lesser_terms(
        haloed, local_index, weights, couplings, occupation, SHIFT_HI, column_start
    )
    sigma_rows = lax.psum_scatter(running, "orb", scatter_dimension=2, tiled=True).astype(
        jnp.bfloat16
    )
    return lax.all_to_all(sigma_rows, "atom", split_axis=0, concat_axis=1, tiled=True)


def solution(mesh):
    placed = (
        P(("energy", "atom"), None, "orb", None),
        P(),
        P(),
        P("atom", None),
        P("atom", None),
        P("atom"),
    )
    return jax.shard_map(
        body,
        mesh=mesh,
        in_specs=placed,
        out_specs=P(("energy", "atom"), None, "orb", None),
        check_vma=False,
    )
```

profile of v0, /device:TPU:0, one launch (start us, length us, event | category | flops | bytes accessed | tf_op | source)
XLA Modules:
  0.0 71.7 jit_solution(10395871338476601972)
XLA Ops:
  6.5 0.0 copy-start
  6.5 4.4 %all-to-all-start = ((bf16[1,4,16,128]{3,2,0,1:T(8,128)(2,1)}), bf16[1,4,16,128]{3,2,0,1:T(8,128)(2,1)S(1)}, u32[]{:S(2)}, u32[]{:S(2)}) async-start(bf16[1,4,16,128]{3,2,0,1:T(8,128)(2,1)} %bitcast.89), calls=%async_computation | async-start | bytes 32768 | tf_op jit(solution)/shard_map/all_to_all | solution.py:63
  10.9 0.0 copy-start.3
  10.9 0.0 reduce-scatter.2.cloned.1.call-start
  10.9 0.7 copy-done.3
  11.6 0.0 copy-done
  11.6 0.6 gather_fusion
  12.2 0.1 bitcast_select_fusion.1
  12.3 0.0 copy-start.2
  12.3 0.6 copy-done.2
  13.0 0.0 copy-start.1
  13.0 0.6 copy-done.1
  13.6 0.6 fusion.18
  14.3 0.5 all-to-all-done
  14.8 1.3 %collective-permute-start.1 = (bf16[4,1,16,128]{3,2,0,1:T(8,128)(2,1)S(1)}, bf16[4,1,16,128]{3,2,0,1:T(8,128)(2,1)S(1)}, u32[]{:S(2)}, u32[]{:S(2)}) collective-permute-start(bf16[4,1,16,128]{3,2,0,1:T(8,128)(2,1)S(1)} %bitcast.84), channel_id=1, source_target_pairs={{16,0},{17,1},{18,2},{19,3},{20,4},{21,5},{22,6},{23,7},{24,8},{25... | collective-permute-start | bytes 49160 | tf_op jit(solution)/shard_map/ppermute | solution.py:18
  16.1 4.5 %collective-permute-start = (bf16[4,1,16,128]{3,2,0,1:T(8,128)(2,1)S(1)}, bf16[4,1,16,128]{3,2,0,1:T(8,128)(2,1)S(1)}, u32[]{:S(2)}, u32[]{:S(2)}) collective-permute-start(bf16[4,1,16,128]{3,2,0,1:T(8,128)(2,1)S(1)} %bitcast.85), channel_id=1, source_target_pairs={{0,16},{1,17},{2,18},{3,19},{4,20},{5,21},{6,22},{7,23},{8,24},{9,... | collective-permute-start | bytes 49160 | tf_op jit(solution)/shard_map/ppermute | solution.py:17
  21.3 0.0 collective-permute-done.1
  21.3 0.8 %collective-permute-done = bf16[4,1,16,128]{3,2,0,1:T(8,128)(2,1)S(1)} collective-permute-done((bf16[4,1,16,128]{3,2,0,1:T(8,128)(2,1)S(1)}, bf16[4,1,16,128]{3,2,0,1:T(8,128)(2,1)S(1)}, u32[]{:S(2)}, u32[]{:S(2)}) %collective-permute-start) | collective-permute-done | bytes 16416 | tf_op jit(solution)/shard_map/ppermute | solution.py:17
  22.0 1.3 %collective-permute-start.3 = (bf16[12,1,16,128]{3,2,0,1:T(8,128)(2,1)S(1)}, bf16[12,1,16,128]{3,2,0,1:T(8,128)(2,1)S(1)}, u32[]{:S(2)}, u32[]{:S(2)}) collective-permute-start(bf16[12,1,16,128]{3,2,0,1:T(8,128)(2,1)S(1)} %pad_maximum_fusion.1), channel_id=1, source_target_pairs={{4,0},{8,4},{12,8},{5,1},{9,5},{13,9},{6,2},{10,6},{14,10},{7,3},{... | collective-permute-start | bytes 147464 | tf_op jit(solution)/shard_map/ppermute | solution.py:18
  23.3 3.0 %collective-permute-start.2 = (bf16[12,1,16,128]{3,2,0,1:T(8,128)(2,1)S(1)}, bf16[12,1,16,128]{3,2,0,1:T(8,128)(2,1)S(1)}, u32[]{:S(2)}, u32[]{:S(2)}) collective-permute-start(bf16[12,1,16,128]{3,2,0,1:T(8,128)(2,1)S(1)} %pad_maximum_fusion.1), channel_id=1, source_target_pairs={{0,4},{4,8},{8,12},{1,5},{5,9},{9,13},{2,6},{6,10},{10,14},{3,7},{... | collective-permute-start | bytes 147464 | tf_op jit(solution)/shard_map/ppermute | solution.py:17
  27.6 0.0 collective-permute-done.3
  27.6 0.0 collective-permute-done.2
  27.7 0.6 gather_fusion.1
  28.3 0.1 bitcast_select_fusion
  28.4 1.4 %multiply_convert_fusion.1 = (bf16[4,1,8,16,128]{4,3,0,2,1:T(8,128)(2,1)S(1)}, bf16[4,1,8,16,128]{4,3,0,2,1:T(8,128)(2,1)S(1)}) fusion(bf16[12,1,8,16,128]{4,3,0,2,1:T(8,128)(2,1)S(1)} %bitcast_select_fusion, f32[8]{0:T(128)S(1)} %compare_convert_fusion, f32[]{:T(128)S(6)} %add.46, f32[]{:T(128)} %bitcast.6, f32[]{:T(128)S(6)} %add.49, f32[]{:T(128)} %bitcast.23), kind=kLoop, calls=%fused_computation.15 | loop fusion | flops 917504 | bytes 786480 | tf_op jit(solution)/shard_map/convert_element_type | solution.py:40
  29.8 0.1 reshape.99
  30.0 0.2 fusion
  30.2 0.2 copy.19
  30.4 0.1 reshape.100
  30.6 0.1 reshape.103
  30.7 0.2 fusion.1
  30.9 0.2 copy.22
  31.2 0.1 reshape.104
  31.3 0.7 %convolution_bitcast_fusion = f32[4,128,64]{1,2,0:T(8,128)S(1)} fusion(bf16[4,8,16,128]{3,2,1,0:T(8,128)(2,1)S(1)} %reshape.104, bf16[1,8,1,64,64]{4,3,1,2,0:T(8,128)(2,1)S(1)} %get-tuple-element.10, s32[]{:T(128)S(6)} %select_n.41), kind=kOutput, calls=%fused_computation.6 | convolution fusion | flops 8388608 | bytes 327684 | tf_op jit(solution)/shard_map/aplj,eapjx->ealx/dot_general | solution.py:51
  32.1 1.4 %fusion.3 = f32[4,1,64,128]{3,2,0,1:T(8,128)} fusion(f32[4,128,64]{1,2,0:T(8,128)S(1)} %convolution_bitcast_fusion, bf16[4,8,16,128]{3,2,1,0:T(8,128)(2,1)S(1)} %reshape.100, bf16[1,8,1,64,64]{4,3,1,2,0:T(8,128)(2,1)S(1)} %get-tuple-element.9, s32[]{:T(128)S(6)} %select_n.41), kind=kOutput, calls=%fused_computation.9 | convolution fusion | flops 8421376 | bytes 458756 | tf_op jit(solution)/shard_map/aplj,eapjx->ealx/dot_general | solution.py:51
  33.5 0.0 reduce-scatter.2.cloned.1.call-update
  33.5 23.6 %reduce-scatter.2.cloned.1.call-done = f32[4,1,16,128]{3,2,0,1:T(8,128)} async-done(((f32[4,1,64,128]{3,2,0,1:T(8,128)}), f32[4,1,16,128]{3,2,0,1:T(8,128)}) %reduce-scatter.2.cloned.1.call-update) | async-done | bytes 32784 | tf_op jit(solution)/shard_map/reduce_scatter | solution.py:70
  57.1 0.8 %convert_bitcast_fusion = bf16[4,1,16,128]{3,2,1,0:T(8,128)(2,1)S(1)} fusion(f32[4,1,16,128]{3,2,0,1:T(8,128)} %reduce-scatter.2.cloned.1.call-done), kind=kLoop, calls=%fused_computation.24 | loop fusion | flops 8192 | bytes 49152 | tf_op jit(solution)/shard_map/convert_element_type | solution.py:70
  57.8 6.4 %all_to_all.24 = bf16[4,1,16,128]{3,2,1,0:T(8,128)(2,1)S(1)} all-to-all(bf16[4,1,16,128]{3,2,1,0:T(8,128)(2,1)S(1)} %convert_bitcast_fusion), channel_id=1, replica_groups=mesh['energy'=2,'atom'=4,'orb'=4] {'atom'}, dimensions={0} | all-to-all | bytes 32768 | tf_op jit(solution)/shard_map/all_to_all | solution.py:73
  64.2 0.6 copy.36
  (9 shorter events, 0.1 us)
Async XLA Ops:
  6.5 5.1 %copy-start = (bf16[32,2,64,64]{3,2,1,0:T(8,128)(2,1)S(1)}, bf16[32,2,64,64]{3,2,1,0:T(8,128)(2,1)}, u32[]{:S(2)}) copy-start(bf16[32,2,64,64]{3,2,1,0:T(8,128)(2,1)} %param.8) | copy-start | bytes 1572868
  6.5 8.2 %all-to-all-start = ((bf16[1,4,16,128]{3,2,0,1:T(8,128)(2,1)}), bf16[1,4,16,128]{3,2,0,1:T(8,128)(2,1)S(1)}, u32[]{:S(2)}, u32[]{:S(2)}) async-start(bf16[1,4,16,128]{3,2,0,1:T(8,128)(2,1)} %bitcast.89), calls=%async_computation | async-start | bytes 32768 | tf_op jit(solution)/shard_map/all_to_all | solution.py:63
  10.9 0.7 copy-start.3
  10.9 46.2 %reduce-scatter.2.cloned.1.call-start = ((), (), s32[]{:S(2)}) async-start(), calls=%async_computation.3 | async-start | bytes 163840 | tf_op jit(solution)/shard_map/reduce_scatter | solution.py:70
  12.3 0.7 copy-start.2
  13.0 0.7 copy-start.1
  14.8 6.5 %collective-permute-start.1 = (bf16[4,1,16,128]{3,2,0,1:T(8,128)(2,1)S(1)}, bf16[4,1,16,128]{3,2,0,1:T(8,128)(2,1)S(1)}, u32[]{:S(2)}, u32[]{:S(2)}) collective-permute-start(bf16[4,1,16,128]{3,2,0,1:T(8,128)(2,1)S(1)} %bitcast.84), channel_id=1, source_target_pairs={{16,0},{17,1},{18,2},{19,3},{20,4},{21,5},{22,6},{23,7},{24,8},{25... | collective-permute-start | bytes 49160 | tf_op jit(solution)/shard_map/ppermute | solution.py:18
  16.1 6.0 %collective-permute-start = (bf16[4,1,16,128]{3,2,0,1:T(8,128)(2,1)S(1)}, bf16[4,1,16,128]{3,2,0,1:T(8,128)(2,1)S(1)}, u32[]{:S(2)}, u32[]{:S(2)}) collective-permute-start(bf16[4,1,16,128]{3,2,0,1:T(8,128)(2,1)S(1)} %bitcast.85), channel_id=1, source_target_pairs={{0,16},{1,17},{2,18},{3,19},{4,20},{5,21},{6,22},{7,23},{8,24},{9,... | collective-permute-start | bytes 49160 | tf_op jit(solution)/shard_map/ppermute | solution.py:17
  22.0 5.6 %collective-permute-start.3 = (bf16[12,1,16,128]{3,2,0,1:T(8,128)(2,1)S(1)}, bf16[12,1,16,128]{3,2,0,1:T(8,128)(2,1)S(1)}, u32[]{:S(2)}, u32[]{:S(2)}) collective-permute-start(bf16[12,1,16,128]{3,2,0,1:T(8,128)(2,1)S(1)} %pad_maximum_fusion.1), channel_id=1, source_target_pairs={{4,0},{8,4},{12,8},{5,1},{9,5},{13,9},{6,2},{10,6},{14,10},{7,3},{... | collective-permute-start | bytes 147464 | tf_op jit(solution)/shard_map/ppermute | solution.py:18
  23.3 4.3 %collective-permute-start.2 = (bf16[12,1,16,128]{3,2,0,1:T(8,128)(2,1)S(1)}, bf16[12,1,16,128]{3,2,0,1:T(8,128)(2,1)S(1)}, u32[]{:S(2)}, u32[]{:S(2)}) collective-permute-start(bf16[12,1,16,128]{3,2,0,1:T(8,128)(2,1)S(1)} %pad_maximum_fusion.1), channel_id=1, source_target_pairs={{0,4},{4,8},{8,12},{1,5},{5,9},{9,13},{2,6},{6,10},{10,14},{3,7},{... | collective-permute-start | bytes 147464 | tf_op jit(solution)/shard_map/ppermute | solution.py:17
Sparse Core Ops, SparseCore 0:
  33.6 23.4 reduce-scatter.1
where the time goes:
time: 72.1 us; the launch traced here: 71.7 us
  waiting for transfers between devices  24.9 us (35%)
  between operations  15.5 us (21%)
  starting transfers between devices  14.5 us (20%)
  blocking collectives  6.38 us (9%)
  local copies, waits for them, and re-layouts  5.4 us (7%)
  matrix products  2.58 us (4%)
  other arithmetic  2.42 us (3%)
    reduce_scatter x1, waiting for transfers between devices, body(): lax.psum_scatter(running, 'orb', scatter_dimension=2, tiled=True)  23.6 us
    ppermute x2, starting transfers between devices, extended(): before = lax.ppermute(last, axis, up)  7.58 us
    all_to_all x1, blocking collectives, body(): lax.all_to_all(sigma_rows, 'atom', split_axis=0, concat_axis=1, tiled=True)  6.38 us
    all_to_all x1, starting transfers between devices, body(): lax.all_to_all(green_lesser, 'atom', split_axis=1, concat_axis=0, tiled=T...  4.37 us
    ppermute x2, starting transfers between devices, extended(): after = lax.ppermute(initial, axis, down)  2.57 us
    unnamed x9, local copies, waits for them, and re-layouts  2.53 us
    dot_general x2, matrix products, lesser_terms(): jnp.einsum('aplj,eapjx->ealx', column_part, left_product, preferred_eleme...  2.14 us
  transfers between devices with their start and end apart: 6, of which 3 were waited for; matrix products, arithmetic and copies ran while one was open for 2% of the time, Pallas kernels for 0%

commit v1 on v0

v1 whole, which is shorter than its diff:
```python
import functools
import math

import jax
import jax.numpy as jnp
from jax import lax
from jax.experimental import pallas as pl
from jax.experimental.pallas import tpu as pltpu
from jax.sharding import PartitionSpec as P

SHIFTS = (2, 4)
A_DEV = 1
EA = ("energy", "atom")
ALL = ("energy", "atom", "orb")


def combine(blocks_ref, low, high, low_scale, high_scale, atom):
    below = blocks_ref[low, :, atom].astype(jnp.float32)
    above = blocks_ref[high, :, atom].astype(jnp.float32)
    mixed = (low_scale * below + high_scale * above).astype(jnp.bfloat16)
    return mixed.reshape(-1, mixed.shape[-1])


def sigma_kernel(dense, spacing, nbr_ref, index_ref, count_ref, occ_ref, blocks_ref, couplings_ref, out_ref, mixed_ref):
    atoms, slots = nbr_ref.shape
    energies = blocks_ref.shape[0]
    rows = blocks_ref.shape[3]
    orbital = couplings_ref.shape[-1]
    row_start = pl.multiple_of(lax.axis_index("orb") * rows, rows)
    own = (lax.axis_index("energy") * lax.axis_size("atom") + lax.axis_index("atom")) // spacing

    def side(mode, sign):
        if not dense:
            return 2 * mode + (sign + 1) // 2, jnp.float32(1.0)
        at = own + sign * (SHIFTS[mode] // spacing)
        inside = jnp.logical_and(at >= 0, at < energies)
        return jnp.clip(at, 0, energies - 1), jnp.where(inside, jnp.float32(1.0), jnp.float32(0.0))

    sides = []
    for mode in range(len(SHIFTS)):
        low, low_in = side(mode, -1)
        high, high_in = side(mode, 1)
        occ = occ_ref[mode]
        sides.append((low, high, occ * low_in, (occ + 1.0) * high_in))

    def store_mixed(atom):
        empty = jnp.zeros((orbital, 2 * orbital), jnp.bfloat16)
        first, second = [combine(blocks_ref, *sides[m], atom) for m in range(2)]
        mixed_ref[atom + A_DEV] = jnp.concatenate(
            [jnp.concatenate([first, empty], 1), jnp.concatenate([empty, second], 1)], 0
        )

    def one_atom(atom, window):
        lhs, matrices = [], []
        for p in range(slots):
            block = index_ref[atom, p]
            matrices.append(jnp.concatenate([couplings_ref[block, 0], couplings_ref[block, 1]], 1))
            part = jnp.concatenate(
                [couplings_ref[block, m, pl.ds(row_start, rows), :] for m in range(2)], 1
            )
            used = p < count_ref[atom]
            named = nbr_ref[atom, p] - atom
            lhs.append(
                jnp.concatenate(
                    [
                        jnp.where(jnp.logical_and(used, named == d), part, jnp.zeros_like(part))
                        for d in window
                    ],
                    1,
                )
            )
        lhs = jnp.concatenate(lhs, 0)
        rhs = jnp.concatenate([mixed_ref[atom + d + A_DEV] for d in window], 0)
        half = jnp.dot(lhs, rhs, preferred_element_type=jnp.float32).astype(jnp.bfloat16)
        parts = []
        for c in range(2):
            z = jnp.concatenate(
                [half[:, (2 * m + c) * orbital : (2 * m + c + 1) * orbital] for m in range(2)], 1
            )
            parts.append(jnp.concatenate([z[p * rows : (p + 1) * rows] for p in range(slots)], 1))
        total = lax.dot_general(
            jnp.concatenate(parts, 0),
            jnp.concatenate(matrices, 1),
            (((1,), (1,)), ((), ())),
            preferred_element_type=jnp.float32,
        )
        out_ref[0, atom] = jnp.concatenate([total[:rows], total[rows:]], 1).astype(out_ref.dtype)

    if atoms <= 8:
        for atom in range(atoms):
            store_mixed(atom)
        for atom in range(atoms):
            one_atom(atom, [d for d in range(-A_DEV, A_DEV + 1) if 0 <= atom + d < atoms])
    else:
        for edge in list(range(A_DEV)) + list(range(atoms + A_DEV, atoms + 2 * A_DEV)):
            mixed_ref[edge] = jnp.zeros(mixed_ref.shape[1:], mixed_ref.dtype)
        pl.loop(0, atoms)(store_mixed)
        pl.loop(0, atoms)(lambda atom: one_atom(atom, range(-A_DEV, A_DEV + 1)))


def gathered_blocks(green, energies, spacing, orb):
    if energies <= 2 * max(SHIFTS):
        groups = [
            [e * orb + o for e in range(c, energies, spacing) for o in range(orb)]
            for c in range(spacing)
        ]
        copies = jnp.broadcast_to(green, (len(groups[0]),) + green.shape[1:])
        got = lax.all_to_all(copies, ALL, 0, 0, axis_index_groups=groups, tiled=True)
        return True, got.reshape((energies // spacing, orb) + green.shape[1:])
    shares = lax.all_gather(green[0], "orb")
    got = [
        lax.ppermute(shares, EA, [(e, e - s) for e in range(energies) if 0 <= e - s < energies])
        for shift in SHIFTS
        for s in (-shift, shift)
    ]
    return False, jnp.stack(got)


def body(energies, orb, green_lesser, occupation, coupling_blocks, neighbours, coupling_index, neighbour_count):
    spacing = math.gcd(*SHIFTS)
    dense, blocks = gathered_blocks(green_lesser, energies, spacing, orb)
    slots = neighbours.shape[1]
    table = jnp.concatenate([neighbours, coupling_index, neighbour_count[:, None]], 1)
    table = lax.all_gather(table, "atom", tiled=True)
    atoms = table.shape[0]
    orbital = coupling_blocks.shape[-1]
    smem = pl.BlockSpec(memory_space=pltpu.SMEM)
    vmem = pl.BlockSpec(memory_space=pltpu.VMEM)
    return pl.pallas_call(
        functools.partial(sigma_kernel, dense, spacing),
        out_shape=jax.ShapeDtypeStruct(green_lesser.shape, green_lesser.dtype),
        in_specs=[smem, smem, smem, smem, vmem, vmem],
        out_specs=vmem,
        scratch_shapes=[pltpu.VMEM((atoms + 2 * A_DEV, 2 * orbital, 4 * orbital), jnp.bfloat16)],
        compiler_params=pltpu.CompilerParams(vmem_limit_bytes=32 * 1024 * 1024),
    )(
        table[:, :slots],
        table[:, slots : 2 * slots],
        table[:, 2 * slots],
        occupation,
        blocks,
        coupling_blocks,
    )


def solution(mesh):
    orb = mesh.shape["orb"]
    energies = mesh.shape["energy"] * mesh.shape["atom"]
    placed = (
        P(EA, None, "orb", None),
        P(),
        P(),
        P("atom", None),
        P("atom", None),
        P("atom"),
    )
    return jax.shard_map(
        functools.partial(body, energies, orb),
        mesh=mesh,
        in_specs=placed,
        out_specs=P(EA, None, "orb", None),
        check_vma=False,
    )
```

time: 72.1 us -> 24.6 us (0.34)
  waiting for transfers between devices: 24.9 us -> 3.86 us
  between operations: 15.5 us -> 0.68 us
  starting transfers between devices: 14.5 us -> 8.31 us
  matrix products: 2.58 us -> 0 us
  other arithmetic: 2.42 us -> 0.07 us
  Pallas kernels: 0 us -> 1.95 us
  blocking collectives: 6.38 us -> 5.06 us
  local copies, waits for them, and re-layouts: 5.4 us -> 4.25 us
    reduce_scatter x1 -> x0, waiting for transfers between devices: 23.6 us -> none  [body(): lax.psum_scatter(running, 'orb', scatter_dimension=2, tiled=True)]
    ppermute x4 -> x0, starting transfers between devices: 10.1 us -> none  [the longest x2 7.58 us: extended(): before = lax.ppermute(last, axis, up)]
    all_to_all x1 -> x0, blocking collectives: 6.38 us -> none  [body(): lax.all_to_all(sigma_rows, 'atom', split_axis=0, concat_axis=1, tiled=True)]
    all_gather x0 -> x1, blocking collectives: none -> 5.06 us  [body(): table = lax.all_gather(table, 'atom', tiled=True)]
    all_to_all x1, starting transfers between devices: 4.37 us -> 8.31 us  [gathered_blocks(): lax.all_to_all(copies, ALL, 0, 0, axis_index_groups=groups, tiled=True)]
    all_to_all x1, waiting for transfers between devices: 0.5 us -> 3.86 us  [gathered_blocks(): lax.all_to_all(copies, ALL, 0, 0, axis_index_groups=groups, tiled=True)]
    dot_general x4 -> x0, matrix products: 2.58 us -> none  [the longest x2 2.14 us: lesser_terms(): jnp.einsum('aplj,eapjx->ealx', column_part, left_product, preferred_eleme...]
    convert_element_type x3 -> x0, other arithmetic: 2.16 us -> none  [the longest x1 1.4 us: lesser_terms(): combined.astype(jnp.bfloat16)]
  transfers between devices with their start and end apart: 6 -> 1, of which waited for: 3 -> 1; matrix products, arithmetic and copies ran while one was open for 2% -> 1% of each run, Pallas kernels for 0% -> 0%
where the time goes in v1:
time: 24.6 us; the launch traced here: 24.2 us
  starting transfers between devices  8.31 us (34%)
  blocking collectives  5.06 us (21%)
  local copies, waits for them, and re-layouts  4.25 us (17%)
  waiting for transfers between devices  3.86 us (16%)
  Pallas kernels  1.95 us (8%)
  between operations  0.68 us (3%)
    all_to_all x1, starting transfers between devices, gathered_blocks(): lax.all_to_all(copies, ALL, 0, 0, axis_index_groups=groups, tiled=True)  8.31 us
    all_gather x1, blocking collectives, body(): table = lax.all_gather(table, 'atom', tiled=True)  5.06 us
    all_to_all x1, waiting for transfers between devices, gathered_blocks(): lax.all_to_all(copies, ALL, 0, 0, axis_index_groups=groups, tiled=True)  3.86 us
    unnamed x8, local copies, waits for them, and re-layouts  2.54 us
    pallas_call x1, Pallas kernels, body(): pl.pallas_call(functools.partial(sigma_kernel, dense, spacing), out_shape...  1.95 us
    broadcast_in_dim x1, local copies, waits for them, and re-layouts, gathered_blocks(): copies = jnp.broadcast_to(green, (len(groups[0]),) + green.shape[1:])  1.46 us
  transfers between devices with their start and end apart: 1, of which 1 were waited for; matrix products, arithmetic and copies ran while one was open for 1% of the time, Pallas kernels for 0%

profile of v1, /device:TPU:0, one launch (start us, length us, event | category | flops | bytes accessed | tf_op | source)
XLA Modules:
  0.0 24.2 jit_solution(1987766193225765021)
XLA Ops:
  0.0 1.5 %broadcast_in_dim.12 = bf16[16,4,16,128]{3,2,1,0:T(8,128)(2,1)} broadcast(bf16[4,16,128]{2,1,0:T(8,128)(2,1)} %bitcast.10), dimensions={1,2,3} | broadcast | bytes 278528 | tf_op jit(solution)/shard_map/broadcast_in_dim | solution.py:107
  1.5 8.3 %all-to-all-start = ((bf16[16,4,16,128]{3,2,1,0:T(8,128)(2,1)}), bf16[16,4,16,128]{3,2,1,0:T(8,128)(2,1)S(1)}, u32[]{:S(2)}, u32[]{:S(2)}) async-start(bf16[16,4,16,128]{3,2,1,0:T(8,128)(2,1)} %broadcast_in_dim.12), calls=%async_computation | async-start | bytes 524288 | tf_op jit(solution)/shard_map/all_to_all | solution.py:108
  10.4 0.0 copy-start.2
  10.4 0.0 copy-start.3
  10.5 0.6 %copy-done.2 = s32[1,8]{1,0:T(1,128)S(1)} copy-done((s32[1,8]{1,0:T(1,128)S(1)}, s32[1,8]{1,0:T(1,128)}, u32[]{:S(2)}) %copy-start.2) | copy-done | bytes 56
  11.1 0.0 copy-done.3
  11.1 0.1 add_bitcast_fusion
  11.2 5.1 %all-gather = s32[4,1,17]{2,1,0:T(1,128)S(1)} all-gather(s32[1,1,17]{2,1,0:T(1,128)S(1)} %add_bitcast_fusion), channel_id=1, replica_groups=mesh['energy'=2,'atom'=4,'orb'=4] {'atom'}, dimensions={0}, use_global_device_ids=true | all-gather | bytes 340 | tf_op jit(solution)/shard_map/all_gather | solution.py:124
  16.2 0.2 slice_reduce_fusion.count_ref
  16.4 0.1 fusion
  16.5 3.9 %all-to-all-done = bf16[16,4,16,128]{3,2,1,0:T(8,128)(2,1)S(1)} async-done(((bf16[16,4,16,128]{3,2,1,0:T(8,128)(2,1)}), bf16[16,4,16,128]{3,2,1,0:T(8,128)(2,1)S(1)}, u32[]{:S(2)}, u32[]{:S(2)}) %all-to-all-start) | async-done | bytes 262176 | tf_op jit(solution)/shard_map/all_to_all | solution.py:108
  20.4 0.0 copy-start.1
  20.4 0.7 %copy-done.1 = f32[2]{0:T(128)S(1)} copy-done((f32[2]{0:T(128)S(1)}, f32[2]{0:T(128)}, u32[]{:S(2)}) %copy-start.1) | copy-done | bytes 32
  21.0 0.0 copy-start
  21.0 1.2 %copy-done = bf16[32,2,64,64]{3,2,1,0:T(8,128)(2,1)S(1)} copy-done((bf16[32,2,64,64]{3,2,1,0:T(8,128)(2,1)S(1)}, bf16[32,2,64,64]{3,2,1,0:T(8,128)(2,1)}, u32[]{:S(2)}) %copy-start) | copy-done | bytes 524312
  22.2 2.0 %shard_map.64 = bf16[1,4,16,128]{3,2,1,0:T(8,128)(2,1)} custom-call(s32[4,8]{1,0:T(4,128)S(1)} %get-tuple-element.6.nbr_ref, s32[4,8]{1,0:T(4,128)S(1)} %get-tuple-element.5.index_ref, s32[4]{0:T(128)S(1)} %slice_reduce_fusion.count_ref, f32[2]{0:T(128)S(1)} %copy-done.1, bf16[4,4,4,16,128]{4,3,2,1,0:T(8,128)(2,1)S(1)} %bitcast.7, ...), custom_call_target="tpu_custom_call" | custom-call | tf_op jit(solution)/shard_map/pallas_call | solution.py:129
Async XLA Ops:
  1.5 18.9 %all-to-all-start = ((bf16[16,4,16,128]{3,2,1,0:T(8,128)(2,1)}), bf16[16,4,16,128]{3,2,1,0:T(8,128)(2,1)S(1)}, u32[]{:S(2)}, u32[]{:S(2)}) async-start(bf16[16,4,16,128]{3,2,1,0:T(8,128)(2,1)} %broadcast_in_dim.12), calls=%async_computation | async-start | bytes 524288 | tf_op jit(solution)/shard_map/all_to_all | solution.py:108
  10.4 0.7 %copy-start.2 = (s32[1,8]{1,0:T(1,128)S(1)}, s32[1,8]{1,0:T(1,128)}, u32[]{:S(2)}) copy-start(s32[1,8]{1,0:T(1,128)} %param.10) | copy-start | bytes 100
  10.4 0.7 %copy-start.3 = (s32[1,8]{1,0:T(1,128)S(1)}, s32[1,8]{1,0:T(1,128)}, u32[]{:S(2)}) copy-start(s32[1,8]{1,0:T(1,128)} %param.9) | copy-start | bytes 100
  20.4 0.7 %copy-start.1 = (f32[2]{0:T(128)S(1)}, f32[2]{0:T(128)}, u32[]{:S(2)}) copy-start(f32[2]{0:T(128)} %occ_ref.1) | copy-start | bytes 28
  21.0 1.2 %copy-start = (bf16[32,2,64,64]{3,2,1,0:T(8,128)(2,1)S(1)}, bf16[32,2,64,64]{3,2,1,0:T(8,128)(2,1)}, u32[]{:S(2)}) copy-start(bf16[32,2,64,64]{3,2,1,0:T(8,128)(2,1)} %couplings_ref.1) | copy-start | bytes 1572868

commit v2 on v1

v2 whole, which is shorter than its diff:
```python
import functools
import math

import jax
import jax.numpy as jnp
from jax import lax
from jax.experimental import pallas as pl
from jax.experimental.pallas import tpu as pltpu
from jax.sharding import PartitionSpec as P

SHIFTS = (2, 4)
MODES = len(SHIFTS)
A_DEV = 1
WINDOW = range(-A_DEV, A_DEV + 1)
EA = ("energy", "atom")
ALL = ("energy", "atom", "orb")
SMEM = pl.BlockSpec(memory_space=pltpu.SMEM)
VMEM = pl.BlockSpec(memory_space=pltpu.VMEM)
ANY = pl.BlockSpec(memory_space=pl.ANY)
VMEM_LIMIT = 32 * 1024 * 1024


def in_hbm(array):
    return pltpu.with_memory_space_constraint(array, pltpu.HBM)


def each_atom(atoms, step):
    if atoms <= 8:
        for atom in range(atoms):
            step(atom)
    else:
        pl.loop(0, atoms)(step)


def copies_kernel(green_ref, couplings_ref, copies_ref, held_ref, own_ref, sems):
    members = copies_ref.shape[0]
    own = pltpu.make_async_copy(green_ref.at[0], own_ref, sems.at[members])
    own.start()
    fetch = pltpu.make_async_copy(couplings_ref, held_ref, sems.at[members + 1])
    fetch.start()
    own.wait()
    copies = [
        pltpu.make_async_copy(own_ref, copies_ref.at[k], sems.at[k]) for k in range(members)
    ]
    for copy in copies:
        copy.start()
    for copy in [*copies, fetch]:
        copy.wait()


def energy_position(spacing):
    return (lax.axis_index("energy") * lax.axis_size("atom") + lax.axis_index("atom")) // spacing


def prepare_kernel(peers, positions, spacing, *refs):
    *tables, occ_ref, couplings_ref, left_ref, stack_ref, factor_ref = refs
    for mode, shift in enumerate(SHIFTS):
        for k, sign in enumerate((-1, 1)):
            factor = occ_ref[mode] + float(k)
            if positions:
                at = energy_position(spacing) + sign * (shift // spacing)
                factor = jnp.where(jnp.logical_and(at >= 0, at < positions), factor, 0.0)
            factor_ref[2 * mode + k] = jnp.full(factor_ref.shape[1:], factor, jnp.float32)
    slots = stack_ref.shape[2] // (2 * couplings_ref.shape[-1])
    rows = left_ref.shape[1] // slots
    lanes = MODES * couplings_ref.shape[-1]
    row_start = pl.multiple_of(lax.axis_index("orb") * rows, rows)

    def prepare(atom, entry):
        count = entry(2, 0)
        for p in range(slots):
            block = entry(1, p)
            stack_ref[atom, :, p * lanes : (p + 1) * lanes] = jnp.concatenate(
                [couplings_ref[block, m] for m in range(MODES)], 1
            )
            part = jnp.concatenate(
                [couplings_ref[block, m, pl.ds(row_start, rows), :] for m in range(MODES)], 1
            )
            place = jnp.where(p < count, entry(0, p) - atom, A_DEV + 1)
            for k, d in enumerate(WINDOW):
                left_ref[atom, p * rows : (p + 1) * rows, k * lanes : (k + 1) * lanes] = jnp.where(
                    place == d, part, jnp.zeros_like(part)
                )

    if peers:
        me = lax.axis_index("atom")
        for k, table_ref in enumerate(tables):
            prepare(me ^ k, lambda row, p, t=table_ref: t[row, p])
    else:
        (table_ref,) = tables
        pl.loop(0, left_ref.shape[0])(lambda a: prepare(a, lambda row, p: table_ref[a, row, p]))


def sigma_kernel(dense, spacing, factor_ref, blocks_ref, left_ref, stack_ref, out_ref, mixed_ref):
    energies, shares, atoms, rows, _ = blocks_ref.shape
    orbital = rows * shares
    slots = left_ref.shape[1] // rows
    lanes = MODES * orbital

    def place(mode, k):
        if not dense:
            return 2 * mode + k
        at = energy_position(spacing) + (2 * k - 1) * (SHIFTS[mode] // spacing)
        return jnp.clip(at, 0, energies - 1)

    sides = [
        (place(m, 0), place(m, 1), factor_ref[2 * m], factor_ref[2 * m + 1]) for m in range(MODES)
    ]

    def combine(atom):
        empty = jnp.zeros((orbital, 2 * orbital), jnp.bfloat16)
        mixed = []
        for low, high, low_scale, high_scale in sides:
            parts = [
                (
                    low_scale * blocks_ref[low, o, atom].astype(jnp.float32)
                    + high_scale * blocks_ref[high, o, atom].astype(jnp.float32)
                ).astype(jnp.bfloat16)
                for o in (range(shares - 1, -1, -1) if dense else range(shares))
            ]
            mixed.append(jnp.concatenate(parts, 0))
        mixed_ref[atom + A_DEV] = jnp.concatenate(
            [jnp.concatenate([mixed[0], empty], 1), jnp.concatenate([empty, mixed[1]], 1)], 0
        )

    def one_atom(atom):
        window = [d for d in WINDOW if atoms > 8 or 0 <= atom + d < atoms]
        first, last = window[0] + A_DEV, window[-1] + A_DEV + 1
        rhs = jnp.concatenate([mixed_ref[atom + d + A_DEV] for d in window], 0)
        half = jnp.dot(
            left_ref[atom, :, first * lanes : last * lanes], rhs, preferred_element_type=jnp.float32
        ).astype(jnp.bfloat16)
        parts = []
        for c in range(2):
            z = jnp.concatenate(
                [half[:, (2 * m + c) * orbital : (2 * m + c + 1) * orbital] for m in range(MODES)], 1
            )
            parts.append(jnp.concatenate([z[p * rows : (p + 1) * rows] for p in range(slots)], 1))
        total = lax.dot_general(
            jnp.concatenate(parts, 0),
            stack_ref[atom],
            (((1,), (1,)), ((), ())),
            preferred_element_type=jnp.float32,
        )
        out_ref[0, atom] = jnp.concatenate([total[:rows], total[rows:]], 1).astype(out_ref.dtype)

    if atoms > 8:
        for edge in list(range(A_DEV)) + list(range(atoms + A_DEV, atoms + 2 * A_DEV)):
            mixed_ref[edge] = jnp.zeros(mixed_ref.shape[1:], mixed_ref.dtype)
    each_atom(atoms, combine)
    each_atom(atoms, one_atom)


def body(energies, orb, green_lesser, occupation, coupling_blocks, neighbours, coupling_index, neighbour_count):
    spacing = math.gcd(*SHIFTS)
    _, atoms, rows, width = green_lesser.shape
    slots = neighbours.shape[1]
    orbital = coupling_blocks.shape[-1]
    lanes = MODES * orbital
    peers = lax.axis_size("atom")
    dense = energies <= 2 * max(SHIFTS)
    swap = peers <= 4 and peers & (peers - 1) == 0 and peers == atoms
    params = pltpu.CompilerParams(vmem_limit_bytes=VMEM_LIMIT)

    groups = [
        [e * orb + o for e in range(c, energies, spacing) for o in range(orb - 1, -1, -1)]
        for c in range(spacing)
    ]
    members = len(groups[0]) if dense else 1
    copies, couplings = pl.pallas_call(
        copies_kernel,
        out_shape=(
            jax.ShapeDtypeStruct((members, atoms, rows, width), green_lesser.dtype),
            pltpu.VMEM(coupling_blocks.shape, coupling_blocks.dtype),
        ),
        in_specs=[ANY, ANY],
        out_specs=(ANY, VMEM),
        scratch_shapes=[
            pltpu.VMEM((atoms, rows, width), green_lesser.dtype),
            pltpu.SemaphoreType.DMA((members + 2,)),
        ],
        compiler_params=params,
    )(in_hbm(green_lesser), in_hbm(coupling_blocks))
    table = jnp.concatenate(
        [neighbours, coupling_index, jnp.broadcast_to(neighbour_count[:, None], (1, slots))], 0
    )

    if dense:
        got = lax.all_to_all(copies, ALL, 0, 0, axis_index_groups=groups, tiled=True)
        blocks = got.reshape(energies // spacing, orb, atoms, rows, width)
    else:
        shares = lax.all_gather(green_lesser[0], "orb")
        blocks = jnp.stack(
            [
                lax.ppermute(shares, EA, [(e, e - s) for e in range(energies) if 0 <= e - s < energies])
                for shift in SHIFTS
                for s in (-shift, shift)
            ]
        )
    if swap:
        tables = [table] + [
            lax.ppermute(table, "atom", [(i, i ^ k) for i in range(peers)]) for k in range(1, peers)
        ]
    else:
        tables = [lax.all_gather(table, "atom")]

    left, stack, factors = pl.pallas_call(
        functools.partial(
            prepare_kernel, peers if swap else 0, energies // spacing if dense else 0, spacing
        ),
        out_shape=(
            jax.ShapeDtypeStruct((atoms, slots * rows, len(WINDOW) * lanes), jnp.bfloat16),
            jax.ShapeDtypeStruct((atoms, orbital, slots * lanes), jnp.bfloat16),
            jax.ShapeDtypeStruct((2 * MODES, rows, width), jnp.float32),
        ),
        in_specs=[SMEM] * (len(tables) + 1) + [VMEM],
        out_specs=(VMEM, VMEM, VMEM),
        compiler_params=params,
    )(*tables, occupation, couplings)

    return pl.pallas_call(
        functools.partial(sigma_kernel, dense, spacing),
        out_shape=jax.ShapeDtypeStruct(green_lesser.shape, green_lesser.dtype),
        in_specs=[VMEM] * 4,
        out_specs=VMEM,
        scratch_shapes=[pltpu.VMEM((atoms + 2 * A_DEV, lanes, 2 * lanes), jnp.bfloat16)],
        compiler_params=params,
    )(factors, blocks, left, stack)


def solution(mesh):
    orb = mesh.shape["orb"]
    energies = mesh.shape["energy"] * mesh.shape["atom"]
    placed = (
        P(EA, None, "orb", None),
        P(),
        P(),
        P("atom", None),
        P("atom", None),
        P("atom"),
    )
    return jax.shard_map(
        functools.partial(body, energies, orb),
        mesh=mesh,
        in_specs=placed,
        out_specs=P(EA, None, "orb", None),
        check_vma=False,
    )
```

time: 24.6 us -> 18.3 us (0.74)
  blocking collectives: 5.06 us -> 0 us
  local copies, waits for them, and re-layouts: 4.25 us -> 0.66 us
  starting transfers between devices: 8.31 us -> 10.7 us
  Pallas kernels: 1.95 us -> 3.79 us
  waiting for transfers between devices: 3.86 us -> 2.08 us
    all_gather x1 -> x0, blocking collectives: 5.06 us -> none  [body(): table = lax.all_gather(table, 'atom', tiled=True)]
    all_to_all x1, waiting for transfers between devices: 3.86 us -> 0.01 us  [body(): lax.all_to_all(copies, ALL, 0, 0, axis_index_groups=groups, tiled=True)]
    pallas_call x0 -> x2, Pallas kernels: none -> 2.5 us  [the longest x1 1.57 us: body(): pl.pallas_call(copies_kernel, out_shape=(jax.ShapeDtypeStruct((members, a...]
    ppermute x0 -> x3, waiting for transfers between devices: none -> 2.08 us  [body(): lax.ppermute(table, 'atom', [(i, i ^ k) for i in range(peers)])]
    unnamed x8 -> x6, local copies, waits for them, and re-layouts: 2.54 us -> 0.59 us
    ppermute x0 -> x3, starting transfers between devices: none -> 1.88 us  [body(): lax.ppermute(table, 'atom', [(i, i ^ k) for i in range(peers)])]
    broadcast_in_dim x1 -> x0, local copies, waits for them, and re-layouts: 1.46 us -> none  [gathered_blocks(): copies = jnp.broadcast_to(green, (len(groups[0]),) + green.shape[1:])]
    pallas_call x1, Pallas kernels: 1.95 us -> 1.29 us  [body(): pl.pallas_call(functools.partial(sigma_kernel, dense, spacing), out_shape...]
  transfers between devices with their start and end apart: 1 -> 4, of which waited for: 1 -> 2; matrix products, arithmetic and copies ran while one was open for 1% -> 1% of each run, Pallas kernels for 0% -> 5%
where the time goes in v2:
time: 18.3 us; the launch traced here: 18 us
  starting transfers between devices  10.7 us (58%)
  Pallas kernels  3.79 us (21%)
  waiting for transfers between devices  2.08 us (11%)
  between operations  0.7 us (4%)
  local copies, waits for them, and re-layouts  0.66 us (4%)
    all_to_all x1, starting transfers between devices, body(): lax.all_to_all(copies, ALL, 0, 0, axis_index_groups=groups, tiled=True)  8.8 us
    ppermute x3, waiting for transfers between devices, body(): lax.ppermute(table, 'atom', [(i, i ^ k) for i in range(peers)])  2.08 us
    ppermute x3, starting transfers between devices, body(): lax.ppermute(table, 'atom', [(i, i ^ k) for i in range(peers)])  1.88 us
    pallas_call x1, Pallas kernels, body(): pl.pallas_call(copies_kernel, out_shape=(jax.ShapeDtypeStruct((members, a...  1.57 us
    pallas_call x1, Pallas kernels, body(): pl.pallas_call(functools.partial(sigma_kernel, dense, spacing), out_shape...  1.29 us
    pallas_call x1, Pallas kernels, body(): pl.pallas_call(functools.partial(prepare_kernel, peers if swap else 0, en...  0.93 us
    unnamed x6, local copies, waits for them, and re-layouts  0.59 us
  transfers between devices with their start and end apart: 4, of which 2 were waited for; matrix products, arithmetic and copies ran while one was open for 1% of the time, Pallas kernels for 5%

profile of v2, /device:TPU:0, one launch (start us, length us, event | category | flops | bytes accessed | tf_op | source)
XLA Modules:
  0.0 18.0 jit_solution(8362190582506592526)
XLA Ops:
  0.0 1.6 %shard_map.64 = (bf16[16,4,16,128]{3,2,1,0:T(8,128)(2,1)}, bf16[32,2,64,64]{3,2,1,0:T(8,128)(2,1)S(1)}) custom-call(bf16[1,4,16,128]{3,2,1,0:T(8,128)(2,1)} %green_ref.1, bf16[32,2,64,64]{3,2,1,0:T(8,128)(2,1)} %couplings_ref.1), custom_call_target="tpu_custom_call" | custom-call | tf_op jit(solution)/shard_map/pallas_call | solution.py:170
  1.6 8.8 %all-to-all-start = ((bf16[16,4,16,128]{3,2,1,0:T(8,128)(2,1)}), bf16[16,4,16,128]{3,2,1,0:T(8,128)(2,1)S(1)}, u32[]{:S(2)}, u32[]{:S(2)}) async-start(bf16[16,4,16,128]{3,2,1,0:T(8,128)(2,1)} %get-tuple-element.12), calls=%async_computation | async-start | bytes 524288 | tf_op jit(solution)/shard_map/all_to_all | solution.py:189
  11.0 0.0 copy-start.1
  11.0 0.0 copy-start.2
  11.1 0.1 pad.2.clone
  11.1 0.6 %copy-done.1 = s32[1,8]{1,0:T(1,128)S(1)} copy-done((s32[1,8]{1,0:T(1,128)S(1)}, s32[1,8]{1,0:T(1,128)}, u32[]{:S(2)}) %copy-start.1) | copy-done | bytes 56
  11.7 0.0 copy-done.2
  11.7 0.1 add_add_fusion.refs_0_
  11.8 0.0 copy-start
  11.8 0.4 %collective-permute-start.2 = (s32[3,8]{1,0:T(4,128)S(1)}, s32[3,8]{1,0:T(4,128)S(1)}, u32[]{:S(2)}, u32[]{:S(2)}) collective-permute-start(s32[3,8]{1,0:T(4,128)S(1)} %add_add_fusion.refs_0_), channel_id=1, source_target_pairs={{0,12},{4,8},{8,4},{12,0},{1,13},{5,9},{9,5},{13,1},{2,14},{6,10},... | collective-permute-start | bytes 296 | tf_op jit(solution)/shard_map/ppermute | solution.py:202
  12.1 1.2 %collective-permute-start.1 = (s32[3,8]{1,0:T(4,128)S(1)}, s32[3,8]{1,0:T(4,128)S(1)}, u32[]{:S(2)}, u32[]{:S(2)}) collective-permute-start(s32[3,8]{1,0:T(4,128)S(1)} %add_add_fusion.refs_0_), channel_id=1, source_target_pairs={{0,8},{4,12},{8,0},{12,4},{1,9},{5,13},{9,1},{13,5},{2,10},{6,14},... | collective-permute-start | bytes 296 | tf_op jit(solution)/shard_map/ppermute | solution.py:202
  13.3 0.3 %collective-permute-start = (s32[3,8]{1,0:T(4,128)S(1)}, s32[3,8]{1,0:T(4,128)S(1)}, u32[]{:S(2)}, u32[]{:S(2)}) collective-permute-start(s32[3,8]{1,0:T(4,128)S(1)} %add_add_fusion.refs_0_), channel_id=1, source_target_pairs={{0,4},{4,0},{8,12},{12,8},{1,5},{5,1},{9,13},{13,9},{2,6},{6,2},{1... | collective-permute-start | bytes 296 | tf_op jit(solution)/shard_map/ppermute | solution.py:202
  13.7 1.4 %collective-permute-done.2.refs_3_ = s32[3,8]{1,0:T(4,128)S(1)} collective-permute-done((s32[3,8]{1,0:T(4,128)S(1)}, s32[3,8]{1,0:T(4,128)S(1)}, u32[]{:S(2)}, u32[]{:S(2)}) %collective-permute-start.2) | collective-permute-done | bytes 128 | tf_op jit(solution)/shard_map/ppermute | solution.py:202
  15.1 0.7 %collective-permute-done.1.refs_2_ = s32[3,8]{1,0:T(4,128)S(1)} collective-permute-done((s32[3,8]{1,0:T(4,128)S(1)}, s32[3,8]{1,0:T(4,128)S(1)}, u32[]{:S(2)}, u32[]{:S(2)}) %collective-permute-start.1) | collective-permute-done | bytes 128 | tf_op jit(solution)/shard_map/ppermute | solution.py:202
  15.7 0.0 collective-permute-done.refs_1_
  15.7 0.0 copy-done
  15.7 0.9 %shard_map.65 = (bf16[4,128,384]{2,1,0:T(8,128)(2,1)S(1)}, bf16[4,64,1024]{2,1,0:T(8,128)(2,1)S(1)}, f32[4,16,128]{2,1,0:T(8,128)S(1)}) custom-call(s32[3,8]{1,0:T(4,128)S(1)} %add_add_fusion.refs_0_, s32[3,8]{1,0:T(4,128)S(1)} %collective-permute-done.refs_1_, s32[3,8]{1,0:T(4,128)S(1)} %collective-permute-done.1.refs_2_, ...), custom_call_target="tpu_custom_call" | custom-call | tf_op jit(solution)/shard_map/pallas_call | solution.py:207
  16.7 0.0 all-to-all-done
  16.7 1.3 %shard_map.66 = bf16[1,4,16,128]{3,2,1,0:T(8,128)(2,1)} custom-call(f32[4,16,128]{2,1,0:T(8,128)S(1)} %get-tuple-element.11.factor_ref, bf16[4,4,4,16,128]{4,3,2,1,0:T(8,128)(2,1)S(1)} %bitcast.2, bf16[4,128,384]{2,1,0:T(8,128)(2,1)S(1)} %get-tuple-element.13.left_ref, bf16[4,64,1024]{2,1,0:T(8,128)(2,1)S(1)} %get-tuple-element.14.stack_ref), custom_call_target="tpu_custom_call" | custom-call | tf_op jit(solution)/shard_map/pallas_call | solution.py:221
Async XLA Ops:
  1.6 15.1 %all-to-all-start = ((bf16[16,4,16,128]{3,2,1,0:T(8,128)(2,1)}), bf16[16,4,16,128]{3,2,1,0:T(8,128)(2,1)S(1)}, u32[]{:S(2)}, u32[]{:S(2)}) async-start(bf16[16,4,16,128]{3,2,1,0:T(8,128)(2,1)} %get-tuple-element.12), calls=%async_computation | async-start | bytes 524288 | tf_op jit(solution)/shard_map/all_to_all | solution.py:189
  11.0 0.7 %copy-start.1 = (s32[1,8]{1,0:T(1,128)S(1)}, s32[1,8]{1,0:T(1,128)}, u32[]{:S(2)}) copy-start(s32[1,8]{1,0:T(1,128)} %param.10) | copy-start | bytes 100
  11.0 0.7 %copy-start.2 = (s32[1,8]{1,0:T(1,128)S(1)}, s32[1,8]{1,0:T(1,128)}, u32[]{:S(2)}) copy-start(s32[1,8]{1,0:T(1,128)} %param.9) | copy-start | bytes 100
  11.8 4.0 %copy-start = (f32[2]{0:T(128)S(1)}, f32[2]{0:T(128)}, u32[]{:S(2)}) copy-start(f32[2]{0:T(128)} %refs_4_.1) | copy-start | bytes 28
  11.8 3.3 %collective-permute-start.2 = (s32[3,8]{1,0:T(4,128)S(1)}, s32[3,8]{1,0:T(4,128)S(1)}, u32[]{:S(2)}, u32[]{:S(2)}) collective-permute-start(s32[3,8]{1,0:T(4,128)S(1)} %add_add_fusion.refs_0_), channel_id=1, source_target_pairs={{0,12},{4,8},{8,4},{12,0},{1,13},{5,9},{9,5},{13,1},{2,14},{6,10},... | collective-permute-start | bytes 296 | tf_op jit(solution)/shard_map/ppermute | solution.py:202
  12.1 3.6 %collective-permute-start.1 = (s32[3,8]{1,0:T(4,128)S(1)}, s32[3,8]{1,0:T(4,128)S(1)}, u32[]{:S(2)}, u32[]{:S(2)}) collective-permute-start(s32[3,8]{1,0:T(4,128)S(1)} %add_add_fusion.refs_0_), channel_id=1, source_target_pairs={{0,8},{4,12},{8,0},{12,4},{1,9},{5,13},{9,1},{13,5},{2,10},{6,14},... | collective-permute-start | bytes 296 | tf_op jit(solution)/shard_map/ppermute | solution.py:202
  13.3 2.4 %collective-permute-start = (s32[3,8]{1,0:T(4,128)S(1)}, s32[3,8]{1,0:T(4,128)S(1)}, u32[]{:S(2)}, u32[]{:S(2)}) collective-permute-start(s32[3,8]{1,0:T(4,128)S(1)} %add_add_fusion.refs_0_), channel_id=1, source_target_pairs={{0,4},{4,0},{8,12},{12,8},{1,5},{5,1},{9,13},{13,9},{2,6},{6,2},{1... | collective-permute-start | bytes 296 | tf_op jit(solution)/shard_map/ppermute | solution.py:202
